TPU v7x, 32 devices: a whole 2x2x4 slice. The times are simulated.
32 devices in a mesh: groups: 2 (over x), rows: 8 (over z, y), inner: 2 (over core).
Axes of the slice: x: 2, y: 2, z: 4, core: 2. Of those that a mesh axis runs over, the one named last changes fastest.
Arguments:
- embeddings: bfloat16 [131072, 1536], P(('groups', 'rows'), 'inner'), parts along dimension 0, may hold values from -7 to 7
- centroids: bfloat16 [16, 256, 1536], P(('groups', 'rows'), None, 'inner'), parts along dimension 0, may hold values from -9 to 9
- block_parent: int32 [256], P(('groups', 'rows')), parts along dimension 0, may hold values from 0 to 7, never falling along the last dimension, each value on 1 to 32 neighbouring positions
- block_size: int32 [256], P(('groups', 'rows')), parts along dimension 0, may hold values from 128 to 512
- owner_slot: int32 [16], P('groups'), parts along dimension 0, may hold values from 0 to 7, each once
Outputs:
- refined: bfloat16 [16, 256, 1536], P(('groups', 'rows'), None, 'inner'), parts along dimension 0
- child_mass: float32 [16, 256], P(('groups', 'rows')), parts along dimension 0
There are 2 independent parts, one for each index of `groups`. A program takes and returns all parts, laid end to end along the dimension named above; each array names one. Nothing has to cross between parts.
Inputs may be any that keep to these rules, and one draw needn't show every extreme that they name: `block_parent`: never falling along the blocks; every parent has 1 to 32 blocks, one parent exactly that many. `owner_slot`: each parent's slot once.
All inputs are finite; a program needn't handle non-finite values.
Results may differ from a plain program's by a relative error of at most 0.008.
Values may be sent and summed in bfloat16 or wider, within the bound.
A program may use at most 128 MiB of HBM per device.

v0:
```python
import math

import jax
import jax.numpy as jnp
from jax import lax
from jax.sharding import PartitionSpec as P

ITERS = 2


def on_device(embeddings, centroids, block_parent, block_size, owner_slot):
    blocks = block_parent.shape[0]
    width = embeddings.shape[1]
    total_slots = owner_slot.shape[0]
    block_layout = embeddings.reshape(blocks, -1, width)
    block_rows = block_layout.shape[1]
    scale_factor = 0.5 / math.sqrt(width * lax.axis_size("inner"))
    slot_range = jnp.arange(total_slots, dtype=jnp.int32)
    parent_hot = block_parent[:, None] == slot_range[None, :]
    block_slot = jnp.sum(jnp.where(parent_hot, owner_slot[None, :], 0), axis=1)
    slot_onehot = (block_slot[:, None] == slot_range[None, :]).astype(jnp.float32)
    slot_pick = slot_onehot.astype(jnp.bfloat16)
    valid = (jnp.arange(block_rows, dtype=jnp.int32)[None, :] < block_size[:, None]).astype(
        jnp.float32
    )
    row_square = jnp.sum(jnp.square(block_layout.astype(jnp.float32)), axis=2)
    current = centroids
    shard_mass = jnp.zeros(centroids.shape[:2], jnp.float32)
    for sweep in range(ITERS):
        picked_parent = jnp.einsum(
            "vh,hma->vma",
            slot_pick,
            lax.all_gather(current, "rows", axis=0, tiled=True),
            preferred_element_type=jnp.float32,
        )
        center_square = jnp.sum(jnp.square(picked_parent), axis=2)
        picked_parent = picked_parent.astype(jnp.bfloat16)
        cross_product = jnp.einsum(
            "hvt,hjt->hvj", block_layout, picked_parent, preferred_element_type=jnp.float32
        )
        partial_value = row_square[:, :, None] + center_square[:, None, :] - 2.0 * cross_product
        distance = lax.psum(partial_value, "inner")
        weight_rows = jax.nn.softmax(-scale_factor * distance, axis=2) * valid[:, :, None]
        assign_block_sums = jnp.einsum(
            "wvj,wvc->wjc",
            weight_rows.astype(jnp.bfloat16),
            block_layout,
            preferred_element_type=jnp.float32,
        )
        assign_block_mass = jnp.sum(weight_rows, axis=1)
        slot_sums = jnp.einsum(
            "sz,suc->zuc", slot_onehot, assign_block_sums, precision=lax.Precision.HIGHEST
        )
        slot_mass = jnp.einsum(
            "bq,bk->qk", slot_onehot, assign_block_mass, precision=lax.Precision.HIGHEST
        )
        local_sums = lax.psum_scatter(
            slot_sums.astype(jnp.bfloat16), "rows", scatter_dimension=0, tiled=True
        ).astype(jnp.float32)
        shard_mass = lax.psum_scatter(
            slot_mass.astype(jnp.bfloat16), "rows", scatter_dimension=0, tiled=True
        ).astype(jnp.float32)
        current = (
            (local_sums + current.astype(jnp.float32)) / (shard_mass[:, :, None] + 1.0)
        ).astype(jnp.bfloat16)
    return (current, shard_mass)


def solution(mesh):
    placed = (
        P(("groups", "rows"), "inner"),
        P(("groups", "rows"), None, "inner"),
        P(("groups", "rows")),
        P(("groups", "rows")),
        P("groups"),
    )
    return jax.shard_map(
        on_device,
        mesh=mesh,
        in_specs=placed,
        out_specs=(P(("groups", "rows"), None, "inner"), P(("groups", "rows"), None)),
        check_vma=False,
    )
```

profile of v0, /device:TPU:0, one launch (start us, length us, event | category | flops | bytes accessed | tf_op | source)
XLA Modules:
  0.0 505.7 jit_solution(4604896980554288972)
XLA Ops:
  8.0 7.1 %multiply_reduce_fusion = f32[8192]{0:T(1024)S(1)} fusion(bf16[8192,768]{1,0:T(8,128)(2,1)} %param.5), kind=kLoop, calls=%fused_computation.2 | loop fusion | flops 18866176 | bytes 12615680 | tf_op jit(solution)/shard_map/reduce_sum | solution.py:26
  15.2 58.2 %all-gather.3.cloned.1.call-done = bf16[8,256,768]{2,1,0:T(8,128)(2,1)} async-done(((bf16[1,256,768]{2,1,0:T(8,128)(2,1)}), bf16[8,256,768]{2,1,0:T(8,128)(2,1)}) %all-gather.3.cloned.1.call-update) | async-done | bytes 3145744 | tf_op jit(solution)/shard_map/all_gather | solution.py:33
  73.4 6.3 %fusion.55 = (bf16[16,256,768]{2,0,1:T(8,128)(2,1)}, f32[16,256]{0,1:T(8,128)S(1)}) fusion(bf16[8,256,768]{2,1,0:T(8,128)(2,1)} %all-gather.3.cloned.1.call-done, s32[16]{0:T(128)S(1)} %select_reduce_fusion), kind=kOutput, calls=%fused_computation.62 | convolution fusion | flops 59765120 | bytes 9453632 | tf_op jit(solution)/shard_map/vh,hma->vma/dot_general | solution.py:30
  79.7 15.5 %bitcast_subtract_fusion.1 = f32[16,512,256]{1,2,0:T(8,128)} fusion(f32[16,256]{1,0:T(8,128)S(1)} %copy.21, f32[16,512]{1,0:T(8,128)S(1)} %add.66, bf16[16,512,768]{2,1,0:T(8,128)(2,1)} %bitcast.26, bf16[16,256,768]{2,0,1:T(8,128)(2,1)} %get-tuple-element.8), kind=kOutput, calls=%fused_computation.10 | convolution fusion | flops 3227516928 | bytes 27312128 | tf_op jit(solution)/shard_map/hvt,hjt->hvj/dot_general | solution.py:38
  96.0 36.9 %all-reduce.5.cloned.1.call-done = f32[16,512,256]{1,2,0:T(8,128)} async-done(((f32[16,512,256]{1,2,0:T(8,128)}), f32[16,512,256]{1,2,0:T(8,128)}) %all-reduce.5.cloned.1.call-update) | async-done | bytes 8388624 | tf_op jit(solution)/shard_map/psum | solution.py:42
  132.9 11.6 %fusion.56 = (f32[16,512]{1,0:T(8,128)S(1)}, f32[16,512,256]{1,2,0:T(8,128)}) fusion(f32[16,512,256]{1,2,0:T(8,128)} %all-reduce.5.cloned.1.call-done), kind=kOutput, calls=%fused_computation.63 | output fusion | flops 8388863 | bytes 16809984 | tf_op jit(solution)/shard_map/sub | solution.py:43
  144.6 15.0 %fusion.18 = f32[16,256,768]{2,1,0:T(8,128)} fusion(bf16[16,512,768]{2,1,0:T(8,128)(2,1)} %bitcast.27, f32[16,512,256]{1,2,0:T(8,128)} %get-tuple-element.11, f32[16,512]{1,0:T(8,128)S(1)} %fusion.38, f32[16,512]{1,0:T(8,128)S(1)} %get-tuple-element.10), kind=kOutput, calls=%fused_computation.25 | convolution fusion | flops 3227516928 | bytes 33619968 | tf_op jit(solution)/shard_map/wvj,wvc->wjc/dot_general | solution.py:44
  159.6 16.0 %fusion.28 = bf16[8,256,768]{2,0,1:T(8,128)(2,1)S(1)} fusion(f32[16,256,768]{2,1,0:T(8,128)} %fusion.18, s32[16]{0:T(128)S(1)} %select_reduce_fusion), kind=kOutput, calls=%fused_computation.35 | convolution fusion | flops 303562880 | bytes 15728704 | tf_op jit(solution)/shard_map/sz,suc->zuc/dot_general | solution.py:51
  175.5 2.3 copy.24
  178.5 4.3 fusion.26
  182.9 22.2 %all-reduce = bf16[8,256]{1,0:T(8,128)(2,1)S(1)} all-reduce(bf16[8,256]{1,0:T(8,128)(2,1)S(1)} %convolution_convert_fusion.1), channel_id=3, replica_groups=mesh['groups'=2,'rows'=8,'inner'=2] {'rows'}, use_global_device_ids=true, to_apply=%region_8.9.clone | all-reduce | flops 2048 | bytes 8192
  205.7 47.8 %reduce-scatter.3.cloned.1.call-done = bf16[1,256,768]{2,1,0:T(8,128)(2,1)} async-done(((bf16[8,256,768]{2,1,0:T(8,128)(2,1)}), bf16[1,256,768]{2,1,0:T(8,128)(2,1)}) %reduce-scatter.3.cloned.1.call-update) | async-done | bytes 393232 | tf_op jit(solution)/shard_map/reduce_scatter | solution.py:57
  253.5 1.9 divide_convert_fusion.1
  255.5 60.3 %all-gather.5.cloned.1.call-done = bf16[8,256,768]{2,1,0:T(8,128)(2,1)} async-done(((bf16[1,256,768]{2,1,0:T(8,128)(2,1)}), bf16[8,256,768]{2,1,0:T(8,128)(2,1)}) %all-gather.5.cloned.1.call-update) | async-done | bytes 3145744 | tf_op jit(solution)/shard_map/all_gather | solution.py:33
  315.7 6.5 %fusion.54 = (bf16[16,256,768]{2,0,1:T(8,128)(2,1)}, f32[16,256]{0,1:T(8,128)S(1)}) fusion(bf16[8,256,768]{2,1,0:T(8,128)(2,1)} %all-gather.5.cloned.1.call-done, s32[16]{0:T(128)S(1)} %select_reduce_fusion), kind=kOutput, calls=%fused_computation.61 | convolution fusion | flops 59765120 | bytes 9453632 | tf_op jit(solution)/shard_map/vh,hma->vma/dot_general | solution.py:30
  322.3 15.5 %bitcast_subtract_fusion = f32[16,512,256]{1,2,0:T(8,128)} fusion(f32[16,256]{1,0:T(8,128)S(1)} %copy.26, f32[16,512]{1,0:T(8,128)S(1)} %add.66, bf16[16,512,768]{2,1,0:T(8,128)(2,1)} %bitcast.28, bf16[16,256,768]{2,0,1:T(8,128)(2,1)} %get-tuple-element.6), kind=kOutput, calls=%fused_computation.9 | convolution fusion | flops 3227516928 | bytes 27312128 | tf_op jit(solution)/shard_map/hvt,hjt->hvj/dot_general | solution.py:38
  337.9 37.6 %all-reduce.7.cloned.1.call-done = f32[16,512,256]{1,2,0:T(8,128)} async-done(((f32[16,512,256]{1,2,0:T(8,128)}), f32[16,512,256]{1,2,0:T(8,128)}) %all-reduce.7.cloned.1.call-update) | async-done | bytes 8388624 | tf_op jit(solution)/shard_map/psum | solution.py:42
  375.5 11.6 %fusion.57 = (f32[16,512]{1,0:T(8,128)S(1)}, f32[16,512,256]{1,2,0:T(8,128)}) fusion(f32[16,512,256]{1,2,0:T(8,128)} %all-reduce.7.cloned.1.call-done), kind=kOutput, calls=%fused_computation.64 | output fusion | flops 8388863 | bytes 16809984 | tf_op jit(solution)/shard_map/sub | solution.py:43
  387.1 15.0 %fusion.16 = f32[16,256,768]{2,1,0:T(8,128)} fusion(bf16[16,512,768]{2,1,0:T(8,128)(2,1)} %bitcast.29, f32[16,512,256]{1,2,0:T(8,128)} %get-tuple-element.13, f32[16,512]{1,0:T(8,128)S(1)} %get-tuple-element.12, f32[16,512]{1,0:T(8,128)S(1)} %fusion.38), kind=kOutput, calls=%fused_computation.23 | convolution fusion | flops 3227516928 | bytes 33619968 | tf_op jit(solution)/shard_map/wvj,wvc->wjc/dot_general | solution.py:44
  402.1 16.0 %fusion.31 = bf16[8,256,768]{2,0,1:T(8,128)(2,1)S(1)} fusion(f32[16,256,768]{2,1,0:T(8,128)} %fusion.16, s32[16]{0:T(128)S(1)} %select_reduce_fusion), kind=kOutput, calls=%fused_computation.36 | convolution fusion | flops 303562880 | bytes 15728704 | tf_op jit(solution)/shard_map/sz,suc->zuc/dot_general | solution.py:51
  418.2 2.3 copy.29
  420.4 4.3 fusion.27
  424.9 22.0 %all-reduce.1 = bf16[8,256]{1,0:T(8,128)(2,1)S(1)} all-reduce(bf16[8,256]{1,0:T(8,128)(2,1)S(1)} %convolution_convert_fusion), channel_id=5, replica_groups=mesh['groups'=2,'rows'=8,'inner'=2] {'rows'}, use_global_device_ids=true, to_apply=%region_15.16.clone | all-reduce | flops 2048 | bytes 8192
  448.1 48.5 %reduce-scatter.5.cloned.1.call-done = bf16[1,256,768]{2,1,0:T(8,128)(2,1)} async-done(((bf16[8,256,768]{2,1,0:T(8,128)(2,1)}), bf16[1,256,768]{2,1,0:T(8,128)(2,1)}) %reduce-scatter.5.cloned.1.call-update) | async-done | bytes 393232 | tf_op jit(solution)/shard_map/reduce_scatter | solution.py:57
  (35 shorter events, 6.4 us)
Async XLA Ops:
  7.2 7.9 %copy-start.3 = (s32[8]{0:T(128)S(1)}, s32[8]{0:T(128)}, u32[]{:S(2)}) copy-start(s32[8]{0:T(128)} %param.9) | copy-start | bytes 100
  7.2 7.9 %copy-start.4 = (s32[16]{0:T(128)S(1)}, s32[16]{0:T(128)}, u32[]{:S(2)}) copy-start(s32[16]{0:T(128)} %param.7) | copy-start | bytes 196
  7.2 66.2 %all-gather.3.cloned.1.call-start = ((), (), s32[]{:S(2)}) async-start(), calls=%async_computation.2 | async-start | bytes 3538944 | tf_op jit(solution)/shard_map/all_gather | solution.py:33
  7.9 125.0 %all-reduce.5.cloned.1.call-start = ((), (), s32[]{:S(2)}) async-start(), calls=%async_computation.3 | async-start | bytes 16777216 | tf_op jit(solution)/shard_map/psum | solution.py:42
  95.3 0.7 copy-start.2
  95.3 158.2 %reduce-scatter.3.cloned.1.call-start = ((), (), s32[]{:S(2)}) async-start(), calls=%async_computation.4 | async-start | bytes 3538944 | tf_op jit(solution)/shard_map/reduce_scatter | solution.py:57
  175.5 2.4 copy-start.5
  175.5 78.0 %copy-start.1 = (bf16[1,256,768]{2,1,0:T(8,128)(2,1)S(1)}, bf16[1,256,768]{2,1,0:T(8,128)(2,1)}, u32[]{:S(2)}) copy-start(bf16[1,256,768]{2,1,0:T(8,128)(2,1)} %param.6) | copy-start | bytes 1179652
  177.8 137.9 %all-gather.5.cloned.1.call-start = ((), (), s32[]{:S(2)}) async-start(), calls=%async_computation.5 | async-start | bytes 3538944 | tf_op jit(solution)/shard_map/all_gather | solution.py:33
  255.4 120.1 %all-reduce.7.cloned.1.call-start = ((), (), s32[]{:S(2)}) async-start(), calls=%async_computation.6 | async-start | bytes 16777216 | tf_op jit(solution)/shard_map/psum | solution.py:42
  337.8 158.7 %reduce-scatter.5.cloned.1.call-start = ((), (), s32[]{:S(2)}) async-start(), calls=%async_computation.7 | async-start | bytes 3538944 | tf_op jit(solution)/shard_map/reduce_scatter | solution.py:57
  418.1 78.4 %copy-start = (bf16[1,256,768]{2,1,0:T(8,128)(2,1)S(1)}, bf16[1,256,768]{2,1,0:T(8,128)(2,1)}, u32[]{:S(2)}) copy-start(bf16[1,256,768]{2,1,0:T(8,128)(2,1)} %divide_convert_fusion.1) | copy-start | bytes 1179652
Sparse Core Ops, SparseCore 0:
  10.2 63.1 all-gather.2
  95.4 37.4 all-reduce.4
  177.9 75.5 reduce-scatter.2
  256.1 59.5 all-gather.4
  338.0 37.4 all-reduce.6
  420.6 75.9 reduce-scatter.4
where the time goes:
time: 512 us; the launch traced here: 506 us
  waiting for transfers between devices  290 us (57%)
  matrix products  106 us (21%)
  other arithmetic  44.7 us (9%)
  blocking collectives  44.2 us (9%)
  between operations  14.7 us (3%)
  local copies, waits for them, and re-layouts  5.36 us (1%)
    all_gather x2, waiting for transfers between devices, on_device(): lax.all_gather(current, 'rows', axis=0, tiled=True)  118 us
    reduce_scatter x2, waiting for transfers between devices, on_device(): lax.psum_scatter(slot_sums.astype(jnp.bfloat16), 'rows', scatter_dimensio...  96.3 us
    psum x2, waiting for transfers between devices, on_device(): distance = lax.psum(partial_value, 'inner')  74.5 us
    unnamed x2, blocking collectives  44.2 us
    dot_general x2, matrix products, on_device(): jnp.einsum('sz,suc->zuc', slot_onehot, assign_block_sums, precision=lax.P...  32 us
    dot_general x2, matrix products, on_device(): jnp.einsum('hvt,hjt->hvj', block_layout, picked_parent, preferred_element...  31.1 us
    dot_general x2, matrix products, on_device(): jnp.einsum('wvj,wvc->wjc', weight_rows.astype(jnp.bfloat16), block_layout...  29.9 us
    sub x2, other arithmetic, on_device(): jax.nn.softmax(-scale_factor * distance, axis=2) * valid[:, :, None]  23.3 us
  transfers between devices with their start and end apart: 6, of which 6 were waited for; matrix products, arithmetic and copies ran while one was open for 4% of the time, Pallas kernels for 0%

commit v1 on v0

v1 whole, which is shorter than its diff:
```python
import functools
import math

import jax
import jax.numpy as jnp
from jax import lax
from jax.experimental import pallas as pl
from jax.experimental.pallas import tpu as pltpu
from jax.sharding import PartitionSpec as P

MESH = pl.DeviceIdType.MESH
BF = jnp.bfloat16
F32 = jnp.float32
EXTRA = 128
CHUNK = 32


def kernel(
    n, nslot, nb, reach, full_width,
    slot_ref, size_ref, last_ref, x_hbm, gathered_hbm, out_ref,
    x, table, own, sent, got, resp, acc, macc, seg, msg, near,
    x_sem, t_sem, d_send, d_recv, r_send, r_recv, n_send, n_recv,
):
    me = lax.axis_index("rows")
    core = lax.axis_index("inner")
    other = 1 - core
    rows = x.shape[0] // nb
    half = rows // 2
    kids, width = table.shape[1], table.shape[2]
    scale = 0.5 / math.sqrt(full_width) * math.log2(math.e)
    partner = {"inner": other}
    offsets = [-j for j in range(1, reach + 1)] + [j for j in range(1, reach + 1)]

    def x_copy(b):
        at = pl.ds(pl.multiple_of(b * rows, rows), rows)
        return pltpu.make_async_copy(x_hbm.at[at], x.at[at], x_sem.at[b])

    t_copy = pltpu.make_async_copy(gathered_hbm, table.at[pl.ds(0, nslot)], t_sem)
    t_copy.start()

    @pl.loop(0, nb)
    def _(b):
        x_copy(b).start()

    for i, off in enumerate(offsets):
        @pl.when(jnp.logical_or(me + off < 0, me + off >= n))
        def _():
            near[i] = jnp.full(near.shape[1:], -1.0, BF)

    barrier = pltpu.get_barrier_semaphore()
    pl.semaphore_signal(barrier, inc=1, device_id=partner, device_id_type=MESH)
    peers = 1
    for off in offsets:
        there = jnp.logical_and(me + off >= 0, me + off < n)
        peers = peers + jnp.where(there, 1, 0)

        @pl.when(there)
        def _():
            pl.semaphore_signal(
                barrier, inc=1, device_id={"rows": me + off}, device_id_type=MESH
            )
    pl.semaphore_wait(barrier, peers)

    def dist_copy(b):
        return pltpu.make_async_remote_copy(
            src_ref=sent.at[b], dst_ref=got.at[b], send_sem=d_send.at[b],
            recv_sem=d_recv.at[b], device_id=partner, device_id_type=MESH,
        )

    def resp_copy(b, part):
        return pltpu.make_async_remote_copy(
            src_ref=resp.at[b, part], dst_ref=resp.at[b, part], send_sem=r_send.at[b],
            recv_sem=r_recv.at[b], device_id=partner, device_id_type=MESH,
        )

    nt = (((1,), (1,)), ((), ()))

    def sweep(index_of, first):
        def dist_step(b):
            if first:
                x_copy(b).wait()
            c = table[index_of(b)]
            cf = c.astype(F32)
            square = jnp.sum(cf * cf, axis=1, keepdims=True)
            far = x[pl.ds(pl.multiple_of(b * rows + other * half, half), half), :]
            sent[b] = 2.0 * lax.dot_general(c, far, nt, preferred_element_type=F32) - square
            dist_copy(b).start()
            mine = x[pl.ds(pl.multiple_of(b * rows + core * half, half), half), :]
            own[b] = 2.0 * lax.dot_general(c, mine, nt, preferred_element_type=F32) - square

        def soft_step(b):
            dist_copy(b).wait()
            logit = (own[b] + got[b]) * scale
            e = jnp.exp2(logit - jnp.max(logit, axis=0, keepdims=True))
            place = lax.broadcasted_iota(jnp.int32, (1, half), 1) + core * half
            used = jnp.where(place < size_ref[b], 1.0, 0.0)
            r = e * (used / jnp.sum(e, axis=0, keepdims=True))
            resp[b, core] = r.astype(BF)
            resp_copy(b, core).start()

        def sum_step(b):
            resp_copy(b, core).wait_send()
            resp_copy(b, other).wait_recv()
            r0, r1 = resp[b, 0], resp[b, 1]
            lo = x[pl.ds(pl.multiple_of(b * rows, half), half), :]
            hi = x[pl.ds(pl.multiple_of(b * rows + half, half), half), :]
            mass = jnp.sum(r0.astype(F32) + r1.astype(F32), axis=1, keepdims=True)
            before = slot_ref[jnp.maximum(b - 1, 0)]
            keep = jnp.where(jnp.logical_and(b > 0, slot_ref[b] == before), 1.0, 0.0)
            total = (
                acc[...] * keep
                + jnp.dot(r0, lo, preferred_element_type=F32)
                + jnp.dot(r1, hi, preferred_element_type=F32)
            )
            acc[...] = total
            tally = macc[...] * keep + mass
            macc[...] = tally
            seg[b, :, :width] = total.astype(BF)
            lane = lax.broadcasted_iota(jnp.int32, (kids, EXTRA), 1)
            number = slot_ref[b].astype(F32)
            seg[b, :, width:] = jnp.where(lane < EXTRA // 2, tally, number).astype(BF)

        acc[...] = jnp.zeros_like(acc)
        macc[...] = jnp.zeros_like(macc)
        lag1, lag2 = 3, 6

        @pl.loop(0, nb + lag2)
        def _(step):
            @pl.when(step < nb)
            def _():
                dist_step(step)

            @pl.when(jnp.logical_and(step >= lag1, step < nb + lag1))
            def _():
                soft_step(step - lag1)

            @pl.when(step >= lag2)
            def _():
                sum_step(step - lag2)

    t_copy.wait()
    sweep(lambda b: slot_ref[b], True)

    head, tail = slot_ref[0], slot_ref[nb - 1]
    msg[0] = seg[last_ref[head]]
    msg[1] = seg[nb - 1]

    def near_copy(i, off):
        which = 0 if off < 0 else 1
        there = offsets.index(-off)
        return pltpu.make_async_remote_copy(
            src_ref=msg.at[which], dst_ref=near.at[there], send_sem=n_send.at[i],
            recv_sem=n_recv.at[there], device_id={"rows": me + off}, device_id_type=MESH,
        )

    def arrival(i):
        return pltpu.make_async_remote_copy(
            src_ref=msg.at[0], dst_ref=near.at[i], send_sem=n_send.at[i],
            recv_sem=n_recv.at[i], device_id={"rows": me}, device_id_type=MESH,
        )

    for i, off in enumerate(offsets):
        @pl.when(jnp.logical_and(me + off >= 0, me + off < n))
        def _():
            near_copy(i, off).start()

    table[nslot] = table[head]
    table[nslot + 1] = table[tail]

    def pieces(body):
        @pl.loop(0, kids // CHUNK)
        def _(c):
            body(pl.ds(pl.multiple_of(c * CHUNK, CHUNK), CHUNK))

    @pl.loop(0, nslot)
    def _(q):
        at = last_ref[q]

        def body(r):
            t = seg[at, r, :].astype(F32)
            new = (t[:, :width] + table[q, r, :].astype(F32)) / (t[:, width:width + 1] + 1.0)
            table[q, r, :] = new.astype(BF)

        pieces(body)

    for i, off in enumerate(offsets):
        @pl.when(jnp.logical_and(me + off >= 0, me + off < n))
        def _():
            near_copy(i, off).wait_send()
            arrival(i).wait_recv()

    ID = width + EXTRA // 2
    for which, number in ((0, head), (1, tail)):
        def body(r):
            t = msg[which, r, :].astype(F32)
            total = t[:, :width] + table[nslot + which, r, :].astype(F32)
            mass = t[:, width:width + 1] + 1.0
            for i in range(len(offsets)):
                m = near[i, r, :].astype(F32)
                flag = jnp.where(m[:, ID:ID + 1] == number.astype(F32), 1.0, 0.0)
                total = total + m[:, :width] * flag
                mass = mass + m[:, width:width + 1] * flag
            table[nslot + which, r, :] = (total / mass).astype(BF)

        pieces(body)

    def second(q):
        return jnp.where(q == head, nslot, jnp.where(q == tail, nslot + 1, q))

    sweep(lambda b: second(slot_ref[b]), False)

    @pl.loop(0, nslot)
    def _(q):
        at, where = last_ref[q], second(q)
        present = jnp.where(slot_ref[at] == q, 1.0, 0.0)
        is_head = jnp.where(q == head, 1.0, 0.0)

        def body(r):
            t = seg[at, r, :].astype(F32) * present
            ident = near[0, r, :].astype(F32)[:, ID:ID + 1]
            begun = jnp.where(ident == head.astype(F32), 1.0, 0.0) * is_head
            fold = present * (1.0 - begun)
            out_ref[q, r, :width] = (
                t[:, :width] + fold * table[where, r, :].astype(F32)
            ).astype(BF)
            out_ref[q, r, width:] = t[:, width:].astype(BF)

        pieces(body)


def on_device(embeddings, centroids, block_parent, block_size, owner_slot):
    nb = block_parent.shape[0]
    rows_all, width = embeddings.shape
    kids = centroids.shape[1]
    nslot = owner_slot.shape[0]
    n = lax.axis_size("rows")
    reach = -(-n // 4)
    half = rows_all // nb // 2
    slot_range = jnp.arange(nslot, dtype=jnp.int32)
    block_slot = jnp.sum(
        jnp.where(block_parent[:, None] == slot_range[None, :], owner_slot[None, :], 0), axis=1
    )
    place = jnp.arange(nb, dtype=jnp.int32)
    last = jnp.max(jnp.where(block_slot[:, None] == slot_range[None, :], place[:, None], 0), axis=0)
    gathered = lax.all_gather(centroids, "rows", axis=0, tiled=True)
    smem = pl.BlockSpec(memory_space=pltpu.SMEM)
    anywhere = pl.BlockSpec(memory_space=pl.ANY)
    dma = pltpu.SemaphoreType.DMA
    partial = pl.pallas_call(
        functools.partial(kernel, n, nslot, nb, reach, width * lax.axis_size("inner")),
        out_shape=jax.ShapeDtypeStruct((nslot, kids, width + EXTRA), BF),
        in_specs=[smem, smem, smem, anywhere, anywhere],
        out_specs=pl.BlockSpec(memory_space=pltpu.VMEM),
        scratch_shapes=[
            pltpu.VMEM((rows_all, width), BF),
            pltpu.VMEM((nslot + 2, kids, width), BF),
            pltpu.VMEM((nb, kids, half), F32),
            pltpu.VMEM((nb, kids, half), F32),
            pltpu.VMEM((nb, kids, half), F32),
            pltpu.VMEM((nb, 2, kids, half), BF),
            pltpu.VMEM((kids, width), F32),
            pltpu.VMEM((kids, EXTRA), F32),
            pltpu.VMEM((nb, kids, width + EXTRA), BF),
            pltpu.VMEM((2, kids, width + EXTRA), BF),
            pltpu.VMEM((2 * reach, kids, width + EXTRA), BF),
            dma((nb,)),
            dma,
            dma((nb,)),
            dma((nb,)),
            dma((nb,)),
            dma((nb,)),
            dma((2 * reach,)),
            dma((2 * reach,)),
        ],
        compiler_params=pltpu.CompilerParams(
            collective_id=0, has_side_effects=True, vmem_limit_bytes=60 * 1024 * 1024
        ),
        cost_estimate=pl.CostEstimate(
            flops=8 * rows_all * kids * width, bytes_accessed=embeddings.size * 2,
            transcendentals=2 * rows_all * kids // 2,
        ),
    )(block_slot, block_size, last, embeddings, gathered)
    total = lax.psum_scatter(partial, "rows", scatter_dimension=0, tiled=True).astype(F32)
    shard_mass = total[:, :, width]
    refined = (total[:, :, :width] / (shard_mass[:, :, None] + 1.0)).astype(BF)
    return (refined, shard_mass)


def solution(mesh):
    placed = (
        P(("groups", "rows"), "inner"),
        P(("groups", "rows"), None, "inner"),
        P(("groups", "rows")),
        P(("groups", "rows")),
        P("groups"),
    )
    return jax.shard_map(
        on_device,
        mesh=mesh,
        in_specs=placed,
        out_specs=(P(("groups", "rows"), None, "inner"), P(("groups", "rows"), None)),
        check_vma=False,
    )
```

time: 512 us -> 240 us (0.47); the launches traced: 506 us -> 240 us
  waiting for transfers between devices: 290 us -> 145 us
  matrix products: 106 us -> 0 us
  Pallas kernels: 0 us -> 76.9 us
  blocking collectives: 44.2 us -> 0 us
  other arithmetic: 44.7 us -> 4 us
  local copies, waits for them, and re-layouts: 5.36 us -> 0.01 us
    dot_general x10 -> x0, matrix products: 106 us -> none  [the longest x2 32 us: on_device(): jnp.einsum('sz,suc->zuc', slot_onehot, assign_block_sums, precision=lax.P...]
    pallas_call x0 -> x1, Pallas kernels: none -> 76.9 us  [on_device(): pl.pallas_call(functools.partial(kernel, n, nslot, nb, reach, width * lax...]
    psum x2 -> x0, waiting for transfers between devices: 74.5 us -> none  [on_device(): distance = lax.psum(partial_value, 'inner')]
    all_gather x2 -> x1, waiting for transfers between devices: 118 us -> 64 us  [on_device(): gathered = lax.all_gather(centroids, 'rows', axis=0, tiled=True)]
    unnamed x2 -> x0, blocking collectives: 44.2 us -> none
    sub x2 -> x0, other arithmetic: 23.3 us -> none  [on_device(): jax.nn.softmax(-scale_factor * distance, axis=2) * valid[:, :, None]]
    reduce_scatter x2 -> x1, waiting for transfers between devices: 96.3 us -> 80 us  [on_device(): lax.psum_scatter(partial, 'rows', scatter_dimension=0, tiled=True)]
    reduce_sum x4 -> x1, other arithmetic: 15.8 us -> 0.76 us  [on_device(): jnp.sum(jnp.where(block_parent[:, None] == slot_range[None, :], owner_slo...]
  transfers between devices with their start and end apart: 6 -> 2, of which waited for: 6 -> 2; matrix products, arithmetic and copies ran while one was open for 4% -> 1% of each run, Pallas kernels for 0% -> 0%
where the time goes in v1:
time: 240 us
  waiting for transfers between devices  145 us (60%)
  Pallas kernels  76.9 us (32%)
  between operations  14 us (6%)
  other arithmetic  4 us (2%)
    reduce_scatter x1, waiting for transfers between devices, on_device(): lax.psum_scatter(partial, 'rows', scatter_dimension=0, tiled=True)  80 us
    pallas_call x1, Pallas kernels, on_device(): pl.pallas_call(functools.partial(kernel, n, nslot, nb, reach, width * lax...  76.9 us
    all_gather x1, waiting for transfers between devices, on_device(): gathered = lax.all_gather(centroids, 'rows', axis=0, tiled=True)  64 us
  transfers between devices with their start and end apart: 2, of which 2 were waited for; matrix products, arithmetic and copies ran while one was open for 1% of the time, Pallas kernels for 0%

profile of v1, /device:TPU:0, one launch (start us, length us, event | category | flops | bytes accessed | tf_op | source)
XLA Modules:
  0.0 239.8 jit_solution(3732312963251304413)
XLA Ops:
  7.2 0.0 all-gather.2.cloned.1.call-start
  7.2 0.7 all-gather.2.cloned.1.call-update
  7.9 0.0 reduce-scatter.2.cloned.1.call-start
  7.9 0.8 select_reduce_fusion.1.slot_ref
  8.7 0.0 copy-start
  8.7 0.6 select_reduce_fusion.last_ref
  9.3 64.0 %all-gather.2.cloned.1.call-done.gathered_hbm = bf16[8,256,768]{2,1,0:T(8,128)(2,1)} async-done(((bf16[1,256,768]{2,1,0:T(8,128)(2,1)}), bf16[8,256,768]{2,1,0:T(8,128)(2,1)}) %all-gather.2.cloned.1.call-update) | async-done | bytes 3145744 | tf_op jit(solution)/shard_map/all_gather | solution.py:245
  73.4 0.0 copy-done
  73.4 76.9 %shard_map.68 = bf16[8,256,896]{2,1,0:T(8,128)(2,1)} custom-call(s32[16]{0:T(128)} %copy-done, s32[16]{0:T(128)} %size_ref.1, s32[8]{0:T(128)} %select_reduce_fusion.last_ref, bf16[8192,768]{1,0:T(8,128)(2,1)} %x_hbm.1, bf16[8,256,768]{2,1,0:T(8,128)(2,1)} %all-gather.2.cloned.1.call-done.gathered_hbm), custom_call_target="tpu_custom_call" | custom-call | flops 12884901888 | bytes 12582912 | tf_op jit(solution)/shard_map/pallas_call | solution.py:249
  150.3 0.0 reduce-scatter.2.cloned.1.call-update
  150.3 80.0 %reduce-scatter.2.cloned.1.call-done = bf16[1,256,896]{2,1,0:T(8,128)(2,1)} async-done(((bf16[8,256,896]{2,1,0:T(8,128)(2,1)}), bf16[1,256,896]{2,1,0:T(8,128)(2,1)}) %reduce-scatter.2.cloned.1.call-update) | async-done | bytes 458768 | tf_op jit(solution)/shard_map/reduce_scatter | solution.py:283
  230.3 1.1 convert_element_type.6
  231.4 0.7 slice_reduce_fusion
  232.1 0.9 fusion
Async XLA Ops:
  7.2 66.2 %all-gather.2.cloned.1.call-start = ((), (), s32[]{:S(2)}) async-start(), calls=%async_computation.1 | async-start | bytes 3538944 | tf_op jit(solution)/shard_map/all_gather | solution.py:245
  7.9 222.4 %reduce-scatter.2.cloned.1.call-start = ((), (), s32[]{:S(2)}) async-start(), calls=%async_computation.2 | async-start | bytes 4128768 | tf_op jit(solution)/shard_map/reduce_scatter | solution.py:283
  8.7 64.7 %copy-start = (s32[16]{0:T(128)}, s32[16]{0:T(128)S(1)}, u32[]{:S(2)}) copy-start(s32[16]{0:T(128)S(1)} %select_reduce_fusion.1.slot_ref) | copy-start | bytes 196
Sparse Core Ops, SparseCore 0:
  10.2 63.1 all-gather.1
  150.5 79.7 reduce-scatter.1

commit v2 on v1

--- a/solution.py
+++ b/solution.py
@@ -13,13 +13,15 @@
 F32 = jnp.float32
 EXTRA = 128
 CHUNK = 32
+PARTS = 4
 
 
 def kernel(
     n, nslot, nb, reach, full_width,
-    slot_ref, size_ref, last_ref, x_hbm, gathered_hbm, out_ref,
-    x, table, own, sent, got, resp, acc, macc, seg, msg, near,
+    slot_ref, size_ref, last_ref, x_hbm, c_hbm, out_ref, mass_ref,
+    x, table, own, sent, got, resp, acc, macc, seg, msg, near, ybuf, zbuf, mass_out, mass_in,
     x_sem, t_sem, d_send, d_recv, r_send, r_recv, n_send, n_recv,
+    g_send, g_recv, y_send, y_recv, z_send, z_recv, m_send, m_recv,
 ):
     me = lax.axis_index("rows")
     core = lax.axis_index("inner")
@@ -35,7 +37,11 @@
         at = pl.ds(pl.multiple_of(b * rows, rows), rows)
         return pltpu.make_async_copy(x_hbm.at[at], x.at[at], x_sem.at[b])
 
-    t_copy = pltpu.make_async_copy(gathered_hbm, table.at[pl.ds(0, nslot)], t_sem)
+    nz = n // 2
+    z, y = me // 2, me % 2
+    beside = me + 1 - 2 * y
+    above, below = z < nz - 1, z > 0
+    t_copy = pltpu.make_async_copy(c_hbm.at[0], table.at[me], t_sem)
     t_copy.start()
 
     @pl.loop(0, nb)
@@ -49,17 +55,67 @@
 
     barrier = pltpu.get_barrier_semaphore()
     pl.semaphore_signal(barrier, inc=1, device_id=partner, device_id_type=MESH)
-    peers = 1
-    for off in offsets:
-        there = jnp.logical_and(me + off >= 0, me + off < n)
-        peers = peers + jnp.where(there, 1, 0)
-
-        @pl.when(there)
-        def _():
-            pl.semaphore_signal(
-                barrier, inc=1, device_id={"rows": me + off}, device_id_type=MESH
-            )
-    pl.semaphore_wait(barrier, peers)
+    for off in range(1, n):
+        pl.semaphore_signal(
+            barrier, inc=1, device_id={"rows": lax.rem(me + off, n)}, device_id_type=MESH
+        )
+    pl.semaphore_wait(barrier, n)
+
+    def part(c):
+        return pl.ds(pl.multiple_of(c * (kids // PARTS), kids // PARTS), kids // PARTS)
+
+    def g_copy(way, s, c):
+        to = (me + 2, me - 2, beside)[way]
+        return pltpu.make_async_remote_copy(
+            src_ref=table.at[s, part(c)], dst_ref=table.at[s, part(c)],
+            send_sem=g_send.at[way, s, c], recv_sem=g_recv.at[s, c],
+            device_id={"rows": to}, device_id_type=MESH,
+        )
+
+    def each_shard(do, arrive):
+        @pl.loop(0, PARTS)
+        def _(c):
+            @pl.when(above)
+            def _():
+                do(g_copy(0, me, c))
+
+            @pl.when(below)
+            def _():
+                do(g_copy(1, me, c))
+
+            do(g_copy(2, me, c))
+
+        for h in range(1, nz):
+            @pl.loop(0, PARTS)
+            def _(c):
+                @pl.when(z >= h)
+                def _():
+                    s = me - 2 * h
+                    arrive(s, c)
+
+                    @pl.when(above)
+                    def _():
+                        do(g_copy(0, s, c))
+
+                    do(g_copy(2, s, c))
+
+                @pl.when(z + h < nz)
+                def _():
+                    s = me + 2 * h
+                    arrive(s, c)
+
+                    @pl.when(below)
+                    def _():
+                        do(g_copy(1, s, c))
+
+                    do(g_copy(2, s, c))
+
+    t_copy.wait()
+    each_shard(lambda copy: copy.start(), lambda s, c: g_copy(2, s, c).wait_recv())
+    for j in range(nz):
+        @pl.loop(0, PARTS)
+        def _(c):
+            g_copy(2, 2 * j + 1 - y, c).wait_recv()
 
     def dist_copy(b):
         return pltpu.make_async_remote_copy(
@@ -138,7 +194,6 @@
             def _():
                 sum_step(step - lag2)
 
-    t_copy.wait()
     sweep(lambda b: slot_ref[b], True)
 
     head, tail = slot_ref[0], slot_ref[nb - 1]
@@ -164,6 +219,7 @@
         def _():
             near_copy(i, off).start()
 
+    each_shard(lambda copy: copy.wait_send(), lambda s, c: None)
     table[nslot] = table[head]
     table[nslot + 1] = table[tail]
 
@@ -209,23 +265,131 @@
 
     sweep(lambda b: second(slot_ref[b]), False)
 
-    @pl.loop(0, nslot)
-    def _(q):
+    def mass_copy(to, source):
+        return pltpu.make_async_remote_copy(
+            src_ref=mass_out.at[to], dst_ref=mass_in.at[source], send_sem=m_send.at[to],
+            recv_sem=m_recv.at[source], device_id={"rows": to}, device_id_type=MESH,
+        )
+
+    def make_partial(q):
         at, where = last_ref[q], second(q)
         present = jnp.where(slot_ref[at] == q, 1.0, 0.0)
         is_head = jnp.where(q == head, 1.0, 0.0)
 
         def body(r):
-            t = seg[at, r, :].astype(F32) * present
+            t = seg[at, r, :width].astype(F32) * present
             ident = near[0, r, :].astype(F32)[:, ID:ID + 1]
             begun = jnp.where(ident == head.astype(F32), 1.0, 0.0) * is_head
             fold = present * (1.0 - begun)
-            out_ref[q, r, :width] = (
-                t[:, :width] + fold * table[where, r, :].astype(F32)
-            ).astype(BF)
-            out_ref[q, r, width:] = t[:, width:].astype(BF)
+            table[q, r, :] = (t + fold * table[where, r, :].astype(F32)).astype(BF)
 
         pieces(body)
+        tile = jnp.transpose(seg[at, :, width:].astype(F32)) * present
+        mass_out[q] = tile[:mass_out.shape[1], :].astype(BF)
+
+    def y_copy(j, c):
+        return pltpu.make_async_remote_copy(
+            src_ref=table.at[2 * j + 1 - y, part(c)], dst_ref=ybuf.at[j, part(c)],
+            send_sem=y_send.at[j, c], recv_sem=y_recv.at[j, c],
+            device_id={"rows": beside}, device_id_type=MESH,
+        )
+
+    def z_copy(j, c, to, place):
+        return pltpu.make_async_remote_copy(
+            src_ref=table.at[2 * j + y, part(c)], dst_ref=zbuf.at[place, part(c)],
+            send_sem=z_send.at[j, c], recv_sem=z_recv.at[place, c],
+            device_id={"rows": to}, device_id_type=MESH,
+        )
+
+    def far_first(body):
+        for t in range(nz - 1, 0, -1):
+            @pl.when(z + t < nz)
+            def _():
+                body(t, 1)
+
+            @pl.when(z >= t)
+            def _():
+                body(t, -1)
+
+        body(0, 0)
+
+    def send_beside(t, sign):
+        j = z + sign * t
+        make_partial(2 * j + 1 - y)
+
+        @pl.loop(0, PARTS)
+        def _(c):
+            y_copy(j, c).start()
+
+    far_first(send_beside)
+    far_first(lambda t, sign: make_partial(2 * (z + sign * t) + y))
+    for off in range(1, n):
+        mass_copy(lax.rem(me + off, n), me).start()
+    mass_in[me] = mass_out[me]
+
+    def pass_on(t, sign):
+        j = z + sign * t
+        q = 2 * j + y
+
+        @pl.loop(0, PARTS)
+        def _(c):
+            r = part(c)
+            y_copy(j, c).wait_recv()
+            if t > 0:
+                table[q, r, :] = (table[q, r, :].astype(F32) + ybuf[j, r, :].astype(F32)).astype(BF)
+
+                @pl.when(below if sign > 0 else above)
+                def _():
+                    z_copy(j, c, me, j).wait_recv()
+                    table[q, r, :] = (
+                        table[q, r, :].astype(F32) + zbuf[j, r, :].astype(F32)
+                    ).astype(BF)
+
+                if t == 1 and sign < 0:
+                    z_copy(j, c, me - 2, nz).start()
+                else:
+                    z_copy(j, c, me + 2 * sign, j).start()
+            else:
+                acc[r, :] = table[me, r, :].astype(F32) + ybuf[z, r, :].astype(F32)
+
+    far_first(pass_on)
+    for off in range(1, n):
+        mass_copy(me, lax.rem(me + off, n)).wait_recv()
+    mass = mass_in[0].astype(F32)
+    for s in range(1, n):
+        mass = mass + mass_in[s].astype(F32)
+    mass_ref[...] = mass[:1, :]
+    column = jnp.transpose(jnp.broadcast_to(mass[:1, :], (EXTRA, kids)))
+    macc[...] = column + 1.0
+
+    @pl.loop(0, PARTS)
+    def _(c):
+        r = part(c)
+
+        @pl.when(below)
+        def _():
+            z_copy(z, c, me, z).wait_recv()
+            acc[r, :] = acc[r, :] + zbuf[z, r, :].astype(F32)
+
+        @pl.when(above)
+        def _():
+            z_copy(z, c, me, nz).wait_recv()
+            acc[r, :] = acc[r, :] + zbuf[nz, r, :].astype(F32)
+
+        out_ref[0, r, :] = (acc[r, :] / macc[r, :1]).astype(BF)
+
+    def sent_all(t, sign):
+        j = z + sign * t
+
+        @pl.loop(0, PARTS)
+        def _(c):
+            y_copy(j, c).wait_send()
+            if t > 0:
+                z_copy(j, c, me + 2 * sign, j).wait_send()
+
+    far_first(sent_all)
+    for off in range(1, n):
+        mass_copy(lax.rem(me + off, n), me).wait_send()
 
 
 def on_device(embeddings, centroids, block_parent, block_size, owner_slot):
@@ -234,7 +398,7 @@
     kids = centroids.shape[1]
     nslot = owner_slot.shape[0]
     n = lax.axis_size("rows")
-    reach = -(-n // 4)
+    reach = max(2, -(-n // 4))
     half = rows_all // nb // 2
     slot_range = jnp.arange(nslot, dtype=jnp.int32)
     block_slot = jnp.sum(
@@ -242,15 +406,18 @@
     )
     place = jnp.arange(nb, dtype=jnp.int32)
     last = jnp.max(jnp.where(block_slot[:, None] == slot_range[None, :], place[:, None], 0), axis=0)
-    gathered = lax.all_gather(centroids, "rows", axis=0, tiled=True)
     smem = pl.BlockSpec(memory_space=pltpu.SMEM)
     anywhere = pl.BlockSpec(memory_space=pl.ANY)
     dma = pltpu.SemaphoreType.DMA
-    partial = pl.pallas_call(
+    vmem = pl.BlockSpec(memory_space=pltpu.VMEM)
+    return pl.pallas_call(
         functools.partial(kernel, n, nslot, nb, reach, width * lax.axis_size("inner")),
-        out_shape=jax.ShapeDtypeStruct((nslot, kids, width + EXTRA), BF),
+        out_shape=(
+            jax.ShapeDtypeStruct((1, kids, width), BF),
+            jax.ShapeDtypeStruct((1, kids), F32),
+        ),
         in_specs=[smem, smem, smem, anywhere, anywhere],
-        out_specs=pl.BlockSpec(memory_space=pltpu.VMEM),
+        out_specs=(vmem, vmem),
         scratch_shapes=[
             pltpu.VMEM((rows_all, width), BF),
             pltpu.VMEM((nslot + 2, kids, width), BF),
@@ -263,6 +430,10 @@
             pltpu.VMEM((nb, kids, width + EXTRA), BF),
             pltpu.VMEM((2, kids, width + EXTRA), BF),
             pltpu.VMEM((2 * reach, kids, width + EXTRA), BF),
+            pltpu.VMEM((n // 2, kids, width), BF),
+            pltpu.VMEM((n // 2 + 1, kids, width), BF),
+            pltpu.VMEM((n, 16, kids), BF),
+            pltpu.VMEM((n, 16, kids), BF),
             dma((nb,)),
             dma,
             dma((nb,)),
@@ -271,6 +442,14 @@
             dma((nb,)),
             dma((2 * reach,)),
             dma((2 * reach,)),
+            dma((3, n, PARTS)),
+            dma((n, PARTS)),
+            dma((n // 2, PARTS)),
+            dma((n // 2, PARTS)),
+            dma((n // 2, PARTS)),
+            dma((n // 2 + 1, PARTS)),
+            dma((n,)),
+            dma((n,)),
         ],
         compiler_params=pltpu.CompilerParams(
             collective_id=0, has_side_effects=True, vmem_limit_bytes=60 * 1024 * 1024
@@ -279,11 +458,7 @@
             flops=8 * rows_all * kids * width, bytes_accessed=embeddings.size * 2,
             transcendentals=2 * rows_all * kids // 2,
         ),
-    )(block_slot, block_size, last, embeddings, gathered)
-    total = lax.psum_scatter(partial, "rows", scatter_dimension=0, tiled=True).astype(F32)
-    shard_mass = total[:, :, width]
-    refined = (total[:, :, :width] / (shard_mass[:, :, None] + 1.0)).astype(BF)
-    return (refined, shard_mass)
+    )(block_slot, block_size, last, embeddings, centroids)
 
 
 def solution(mesh):

time: 240 us -> 154 us (0.64)
  waiting for transfers between devices: 145 us -> 0 us
  Pallas kernels: 76.9 us -> 149 us
  between operations: 14 us -> 0.64 us
  local copies, waits for them, and re-layouts: 0.01 us -> 3 us
  other arithmetic: 4 us -> 1.38 us
    reduce_scatter x1 -> x0, waiting for transfers between devices: 80 us -> none  [on_device(): lax.psum_scatter(partial, 'rows', scatter_dimension=0, tiled=True)]
    pallas_call x1, Pallas kernels: 76.9 us -> 149 us  [on_device(): pl.pallas_call(functools.partial(kernel, n, nslot, nb, reach, width * lax...]
    all_gather x1 -> x0, waiting for transfers between devices: 64 us -> none  [on_device(): gathered = lax.all_gather(centroids, 'rows', axis=0, tiled=True)]
    unnamed x2 -> x4, local copies, waits for them, and re-layouts: 0.01 us -> 3 us
  transfers between devices with their start and end apart: 2 -> 0, of which waited for: 2 -> 0; matrix products, arithmetic and copies ran while one was open for 1% -> 0% of each run, Pallas kernels for 0% -> 0%
where the time goes in v2:
time: 154 us
  Pallas kernels  149 us (97%)
  local copies, waits for them, and re-layouts  3 us (2%)
    pallas_call x1, Pallas kernels, on_device(): pl.pallas_call(functools.partial(kernel, n, nslot, nb, reach, width * lax...  149 us

profile of v2, /device:TPU:0, one launch (start us, length us, event | category | flops | bytes accessed | tf_op | source)
XLA Modules:
  0.0 153.8 jit_solution(13751269673109863141)
XLA Ops:
  0.6 0.8 select_reduce_fusion.1.slot_ref
  1.4 0.0 copy-start
  1.4 0.6 select_reduce_fusion.last_ref
  2.0 0.0 copy-done
  2.0 148.7 %shard_map.68 = (bf16[1,256,768]{2,1,0:T(8,128)(2,1)}, f32[1,256]{1,0:T(1,128)}) custom-call(s32[16]{0:T(128)} %copy-done, s32[16]{0:T(128)} %size_ref.1, s32[8]{0:T(128)} %select_reduce_fusion.last_ref, bf16[8192,768]{1,0:T(8,128)(2,1)} %x_hbm.1, bf16[1,256,768]{2,1,0:T(8,128)(2,1)} %c_hbm.1), custom_call_target="tpu_custom_call" | custom-call | flops 12884901888 | bytes 12582912 | tf_op jit(solution)/shard_map/pallas_call | solution.py:413
  150.8 1.8 %copy.9 = bf16[1,256,768]{2,1,0:T(8,128)(2,1)} copy(bf16[1,256,768]{2,1,0:T(8,128)(2,1)} %get-tuple-element.4) | data formatting | bytes 786432
  152.5 1.2 copy.10
Async XLA Ops:
  1.4 0.6 copy-start

commit v3 on v2

--- a/solution.py
+++ b/solution.py
@@ -13,6 +13,7 @@
 F32 = jnp.float32
 EXTRA = 128
 CHUNK = 32
+LAG1, LAG2 = 4, 8
 PARTS = 4
 
 
@@ -132,67 +133,63 @@
     nt = (((1,), (1,)), ((), ()))
 
     def sweep(index_of, first):
-        def dist_step(b):
-            if first:
-                x_copy(b).wait()
-            c = table[index_of(b)]
-            cf = c.astype(F32)
-            square = jnp.sum(cf * cf, axis=1, keepdims=True)
-            far = x[pl.ds(pl.multiple_of(b * rows + other * half, half), half), :]
-            sent[b] = 2.0 * lax.dot_general(c, far, nt, preferred_element_type=F32) - square
-            dist_copy(b).start()
-            mine = x[pl.ds(pl.multiple_of(b * rows + core * half, half), half), :]
-            own[b] = 2.0 * lax.dot_general(c, mine, nt, preferred_element_type=F32) - square
-
-        def soft_step(b):
-            dist_copy(b).wait()
-            logit = (own[b] + got[b]) * scale
-            e = jnp.exp2(logit - jnp.max(logit, axis=0, keepdims=True))
-            place = lax.broadcasted_iota(jnp.int32, (1, half), 1) + core * half
-            used = jnp.where(place < size_ref[b], 1.0, 0.0)
-            r = e * (used / jnp.sum(e, axis=0, keepdims=True))
-            resp[b, core] = r.astype(BF)
-            resp_copy(b, core).start()
-
-        def sum_step(b):
-            resp_copy(b, core).wait_send()
-            resp_copy(b, other).wait_recv()
-            r0, r1 = resp[b, 0], resp[b, 1]
-            lo = x[pl.ds(pl.multiple_of(b * rows, half), half), :]
-            hi = x[pl.ds(pl.multiple_of(b * rows + half, half), half), :]
-            mass = jnp.sum(r0.astype(F32) + r1.astype(F32), axis=1, keepdims=True)
-            before = slot_ref[jnp.maximum(b - 1, 0)]
-            keep = jnp.where(jnp.logical_and(b > 0, slot_ref[b] == before), 1.0, 0.0)
-            total = (
-                acc[...] * keep
-                + jnp.dot(r0, lo, preferred_element_type=F32)
-                + jnp.dot(r1, hi, preferred_element_type=F32)
-            )
-            acc[...] = total
-            tally = macc[...] * keep + mass
-            macc[...] = tally
-            seg[b, :, :width] = total.astype(BF)
-            lane = lax.broadcasted_iota(jnp.int32, (kids, EXTRA), 1)
-            number = slot_ref[b].astype(F32)
-            seg[b, :, width:] = jnp.where(lane < EXTRA // 2, tally, number).astype(BF)
-
         acc[...] = jnp.zeros_like(acc)
         macc[...] = jnp.zeros_like(macc)
-        lag1, lag2 = 3, 6
-
-        @pl.loop(0, nb + lag2)
-        def _(step):
-            @pl.when(step < nb)
-            def _():
-                dist_step(step)
-
-            @pl.when(jnp.logical_and(step >= lag1, step < nb + lag1))
-            def _():
-                soft_step(step - lag1)
-
-            @pl.when(step >= lag2)
-            def _():
-                sum_step(step - lag2)
+
+        def body(dist, soft, summed):
+            if dist is not None:
+                if first:
+                    x_copy(dist).wait()
+                c = table[index_of(dist)]
+                far = x[pl.ds(pl.multiple_of(dist * rows + other * half, half), half), :]
+                mine = x[pl.ds(pl.multiple_of(dist * rows + core * half, half), half), :]
+            if soft is not None:
+                dist_copy(soft).wait()
+                logit = (own[soft] + got[soft]) * scale
+            if summed is not None:
+                resp_copy(summed, core).wait_send()
+                resp_copy(summed, other).wait_recv()
+                r = jnp.concatenate([resp[summed, 0], resp[summed, 1]], axis=1)
+                points = x[pl.ds(pl.multiple_of(summed * rows, rows), rows), :]
+                before = slot_ref[jnp.maximum(summed - 1, 0)]
+                keep = jnp.where(
+                    jnp.logical_and(summed > 0, slot_ref[summed] == before), 1.0, 0.0
+                )
+            if dist is not None:
+                cf = c.astype(F32)
+                square = jnp.sum(cf * cf, axis=1, keepdims=True)
+                away = 2.0 * lax.dot_general(c, far, nt, preferred_element_type=F32) - square
+                sent[dist] = away
+                here = 2.0 * lax.dot_general(c, mine, nt, preferred_element_type=F32) - square
+                own[dist] = here
+            if soft is not None:
+                e = jnp.exp2(logit - jnp.max(logit, axis=0, keepdims=True))
+                place = lax.broadcasted_iota(jnp.int32, (1, half), 1) + core * half
+                used = jnp.where(place < size_ref[soft], 1.0, 0.0)
+                resp[soft, core] = (e * (used / jnp.sum(e, axis=0, keepdims=True))).astype(BF)
+            if summed is not None:
+                total = acc[...] * keep + jnp.dot(r, points, preferred_element_type=F32)
+                acc[...] = total
+                seg[summed, :, :width] = total.astype(BF)
+                tally = macc[...] * keep + jnp.sum(r.astype(F32), axis=1, keepdims=True)
+                macc[...] = tally
+                lane = lax.broadcasted_iota(jnp.int32, (kids, EXTRA), 1)
+                number = slot_ref[summed].astype(F32)
+                seg[summed, :, width:] = jnp.where(lane < EXTRA // 2, tally, number).astype(BF)
+            if dist is not None:
+                dist_copy(dist).start()
+            if soft is not None:
+                resp_copy(soft, core).start()
+
+        marks = sorted({0, LAG1, LAG2, nb, nb + LAG1, nb + LAG2})
+        for lo, hi in zip(marks[:-1], marks[1:]):
+            @pl.loop(lo, hi)
+            def _(step, lo=lo):
+                body(
+                    step if lo < nb else None,
+                    step - LAG1 if LAG1 <= lo < nb + LAG1 else None,
+                    step - LAG2 if LAG2 <= lo else None,
+                )
 
     sweep(lambda b: slot_ref[b], True)
 
@@ -200,24 +197,27 @@
     msg[0] = seg[last_ref[head]]
     msg[1] = seg[nb - 1]
 
-    def near_copy(i, off):
+    def near_copy(i, off, c):
         which = 0 if off < 0 else 1
         there = offsets.index(-off)
         return pltpu.make_async_remote_copy(
-            src_ref=msg.at[which], dst_ref=near.at[there], send_sem=n_send.at[i],
-            recv_sem=n_recv.at[there], device_id={"rows": me + off}, device_id_type=MESH,
-        )
-
-    def arrival(i):
-        return pltpu.make_async_remote_copy(
-            src_ref=msg.at[0], dst_ref=near.at[i], send_sem=n_send.at[i],
-            recv_sem=n_recv.at[i], device_id={"rows": me}, device_id_type=MESH,
-        )
-
-    for i, off in enumerate(offsets):
-        @pl.when(jnp.logical_and(me + off >= 0, me + off < n))
-        def _():
-            near_copy(i, off).start()
+            src_ref=msg.at[which, part(c)], dst_ref=near.at[there, part(c)],
+            send_sem=n_send.at[i, c], recv_sem=n_recv.at[there, c],
+            device_id={"rows": me + off}, device_id_type=MESH,
+        )
+
+    def arrival(i, c):
+        return pltpu.make_async_remote_copy(
+            src_ref=msg.at[0, part(c)], dst_ref=near.at[i, part(c)], send_sem=n_send.at[i, c],
+            recv_sem=n_recv.at[i, c], device_id={"rows": me}, device_id_type=MESH,
+        )
+
+    @pl.loop(0, PARTS)
+    def _(c):
+        for i, off in enumerate(offsets):
+            @pl.when(jnp.logical_and(me + off >= 0, me + off < n))
+            def _():
+                near_copy(i, off, c).start()
 
     each_shard(lambda copy: copy.wait_send(), lambda s, c: None)
     table[nslot] = table[head]
@@ -239,26 +239,29 @@
 
         pieces(body)
 
-    for i, off in enumerate(offsets):
-        @pl.when(jnp.logical_and(me + off >= 0, me + off < n))
-        def _():
-            near_copy(i, off).wait_send()
-            arrival(i).wait_recv()
-
     ID = width + EXTRA // 2
-    for which, number in ((0, head), (1, tail)):
-        def body(r):
-            t = msg[which, r, :].astype(F32)
-            total = t[:, :width] + table[nslot + which, r, :].astype(F32)
-            mass = t[:, width:width + 1] + 1.0
-            for i in range(len(offsets)):
-                m = near[i, r, :].astype(F32)
-                flag = jnp.where(m[:, ID:ID + 1] == number.astype(F32), 1.0, 0.0)
-                total = total + m[:, :width] * flag
-                mass = mass + m[:, width:width + 1] * flag
-            table[nslot + which, r, :] = (total / mass).astype(BF)
-
-        pieces(body)
+
+    @pl.loop(0, PARTS)
+    def _(c):
+        for i, off in enumerate(offsets):
+            @pl.when(jnp.logical_and(me + off >= 0, me + off < n))
+            def _():
+                near_copy(i, off, c).wait_send()
+                arrival(i, c).wait_recv()
+
+        for which, number in ((0, head), (1, tail)):
+            @pl.loop(0, kids // PARTS // 16)
+            def _(k):
+                r = pl.ds(pl.multiple_of(c * (kids // PARTS) + k * 16, 16), 16)
+                t = msg[which, r, :].astype(F32)
+                total = t[:, :width] + table[nslot + which, r, :].astype(F32)
+                mass = t[:, width:width + 1] + 1.0
+                for i in range(len(offsets)):
+                    m = near[i, r, :].astype(F32)
+                    flag = jnp.where(m[:, ID:ID + 1] == number.astype(F32), 1.0, 0.0)
+                    total = total + m[:, :width] * flag
+                    mass = mass + m[:, width:width + 1] * flag
+                table[nslot + which, r, :] = (total / mass).astype(BF)
 
     def second(q):
         return jnp.where(q == head, nslot, jnp.where(q == tail, nslot + 1, q))
@@ -440,8 +443,8 @@
             dma((nb,)),
             dma((nb,)),
             dma((nb,)),
-            dma((2 * reach,)),
-            dma((2 * reach,)),
+            dma((2 * reach, PARTS)),
+            dma((2 * reach, PARTS)),
             dma((3, n, PARTS)),
             dma((n, PARTS)),
             dma((n // 2, PARTS)),

time: 154 us -> 138 us (0.90)
  Pallas kernels: 149 us -> 132 us
    pallas_call x1, Pallas kernels: 149 us -> 132 us  [on_device(): pl.pallas_call(functools.partial(kernel, n, nslot, nb, reach, width * lax...]
where the time goes in v3:
time: 138 us; the launch traced here: 137 us
  Pallas kernels  132 us (96%)
  local copies, waits for them, and re-layouts  3 us (2%)
    pallas_call x1, Pallas kernels, on_device(): pl.pallas_call(functools.partial(kernel, n, nslot, nb, reach, width * lax...  132 us
    unnamed x4, local copies, waits for them, and re-layouts  3 us

profile of v3, /device:TPU:0, one launch (start us, length us, event | category | flops | bytes accessed | tf_op | source)
XLA Modules:
  0.0 137.5 jit_solution(8826814593923933959)
XLA Ops:
  0.6 0.8 select_reduce_fusion.1.slot_ref
  1.4 0.0 copy-start
  1.4 0.6 select_reduce_fusion.last_ref
  2.0 0.0 copy-done
  2.0 132.5 %shard_map.68 = (bf16[1,256,768]{2,1,0:T(8,128)(2,1)}, f32[1,256]{1,0:T(1,128)}) custom-call(s32[16]{0:T(128)} %copy-done, s32[16]{0:T(128)} %size_ref.1, s32[8]{0:T(128)} %select_reduce_fusion.last_ref, bf16[8192,768]{1,0:T(8,128)(2,1)} %x_hbm.1, bf16[1,256,768]{2,1,0:T(8,128)(2,1)} %c_hbm.1), custom_call_target="tpu_custom_call" | custom-call | flops 12884901888 | bytes 12582912 | tf_op jit(solution)/shard_map/pallas_call | solution.py:416
  134.5 1.8 %copy.9 = bf16[1,256,768]{2,1,0:T(8,128)(2,1)} copy(bf16[1,256,768]{2,1,0:T(8,128)(2,1)} %get-tuple-element.4) | data formatting | bytes 786432
  136.3 1.2 copy.10
Async XLA Ops:
  1.4 0.6 copy-start

commit v4 on v3

--- a/solution.py
+++ b/solution.py
@@ -13,7 +13,7 @@
 F32 = jnp.float32
 EXTRA = 128
 CHUNK = 32
-LAG1, LAG2 = 4, 8
+LAG1, LAG2 = 5, 10
 PARTS = 4
 
 
@@ -86,6 +86,32 @@
 
             do(g_copy(2, me, c))
 
+        def crossed(h):
+            @pl.when(z >= h)
+            def _():
+                s = beside - 2 * h
+                arrive(s, 0)
+
+                @pl.when(above)
+                def _():
+                    do(g_copy(0, s, 0))
+
+                if h == 0:
+                    @pl.when(below)
+                    def _():
+                        do(g_copy(1, s, 0))
+
+            if h > 0:
+                @pl.when(z + h < nz)
+                def _():
+                    s = beside + 2 * h
+                    arrive(s, 0)
+
+                    @pl.when(below)
+                    def _():
+                        do(g_copy(1, s, 0))
+
+        crossed(0)
         for h in range(1, nz):
             @pl.loop(0, PARTS)
             def _(c):
@@ -98,7 +124,9 @@
                     def _():
                         do(g_copy(0, s, c))
 
-                    do(g_copy(2, s, c))
+                    @pl.when(c > 0)
+                    def _():
+                        do(g_copy(2, s, c))
 
                 @pl.when(z + h < nz)
                 def _():
@@ -109,12 +137,16 @@
                     def _():
                         do(g_copy(1, s, c))
 
-                    do(g_copy(2, s, c))
+                    @pl.when(c > 0)
+                    def _():
+                        do(g_copy(2, s, c))
+
+            crossed(h)
 
     t_copy.wait()
     each_shard(lambda copy: copy.start(), lambda s, c: g_copy(2, s, c).wait_recv())
     for j in range(nz):
-        @pl.loop(0, PARTS)
+        @pl.loop(1, PARTS)
         def _(c):
             g_copy(2, 2 * j + 1 - y, c).wait_recv()
 

time: 138 us -> 136 us (0.986)
    pallas_call x1, Pallas kernels: 132 us -> 131 us  [on_device(): pl.pallas_call(functools.partial(kernel, n, nslot, nb, reach, width * lax...]
where the time goes in v4:
time: 136 us
  Pallas kernels  131 us (96%)
  local copies, waits for them, and re-layouts  3 us (2%)
  other arithmetic  1.38 us (1%)
    pallas_call x1, Pallas kernels, on_device(): pl.pallas_call(functools.partial(kernel, n, nslot, nb, reach, width * lax...  131 us
    unnamed x4, local copies, waits for them, and re-layouts  3 us

profile of v4, /device:TPU:0, one launch (start us, length us, event | category | flops | bytes accessed | tf_op | source)
XLA Modules:
  0.0 136.1 jit_solution(14920233836452024664)
XLA Ops:
  0.6 0.8 select_reduce_fusion.1.slot_ref
  1.4 0.0 copy-start
  1.4 0.6 select_reduce_fusion.last_ref
  2.0 0.0 copy-done
  2.0 131.1 %shard_map.68 = (bf16[1,256,768]{2,1,0:T(8,128)(2,1)}, f32[1,256]{1,0:T(1,128)}) custom-call(s32[16]{0:T(128)} %copy-done, s32[16]{0:T(128)} %size_ref.1, s32[8]{0:T(128)} %select_reduce_fusion.last_ref, bf16[8192,768]{1,0:T(8,128)(2,1)} %x_hbm.1, bf16[1,256,768]{2,1,0:T(8,128)(2,1)} %c_hbm.1), custom_call_target="tpu_custom_call" | custom-call | flops 12884901888 | bytes 12582912 | tf_op jit(solution)/shard_map/pallas_call | solution.py:448
  133.1 1.8 %copy.9 = bf16[1,256,768]{2,1,0:T(8,128)(2,1)} copy(bf16[1,256,768]{2,1,0:T(8,128)(2,1)} %get-tuple-element.4) | data formatting | bytes 786432
  134.9 1.2 copy.10
Async XLA Ops:
  1.4 0.6 copy-start
